TPU v7x, 32 devices: a whole 2x2x4 slice. The times are simulated.
32 devices in a mesh: req: 8 (over z, x), tp: 4 (over y, core).
Axes of the slice: x: 2, y: 2, z: 4, core: 2. Of those that a mesh axis runs over, the one named last changes fastest.
Arguments:
- queries: bfloat16 [64, 4096], P('req', 'tp'), may hold values from -320 to 320, as said below
- new_kv: bfloat16 [64, 2, 512], P('req', None, 'tp'), may hold values from -6 to 6
- own_kv: bfloat16 [64, 128, 2, 512], P('req', None, None, 'tp'), may hold values from -6 to 6
- prompt_kv: bfloat16 [8, 512, 2, 512], P('req', None, None, 'tp'), may hold values from -6 to 6
- out_weight: bfloat16 [4096, 2048], P('tp'), may hold values from -0.09375 to 0.09375
- parents: int32 [64], replicated, may hold values from 0 to 63, as said below
- own_len: int32 [64], replicated, may hold values from 1 to 128, as said below
- first_beam: int32 [64], replicated, may hold values from 0 to 63, as said below
Outputs:
- mixed_out: bfloat16 [64, 2048], P('req', 'tp')
Inputs may be any that keep to these rules, and one draw needn't show every extreme that they name: Beams of one request are consecutive; first_beam[b] is the first of them; every request but the last holds 8 to 16 beams, and one holds exactly 16. parents[b] is a beam of the same request as b. `own_len`: some beam has exactly 128 valid positions. queries are real-valued, with row scales that may differ widely.
All inputs are finite; a program needn't handle non-finite values.
Results may differ from a plain program's by a relative error of at most 0.015.
Values may be sent and summed in bfloat16 or wider, within the bound.
A program may use at most 64 MiB of HBM per device.

v0:
```python
import jax
import jax.numpy as jnp
from jax import lax
from jax.sharding import PartitionSpec as P

HD = 128
MOST_BEAMS = 16


MASKED_SCORE = -1e30


def from_behind(block, axis, distance):
    devices = range(lax.axis_size(axis))
    route = [(i - distance, i) for i in devices if i - distance in devices]
    return lax.ppermute(block, axis, route)


def partial_block(query_block, key_block, value_block, allowed):
    score_scale = query_block.shape[-1] ** (-0.5)
    scores = jnp.einsum(
        "nkgd,nskd->nkgs", query_block, key_block, preferred_element_type=jnp.float32
    )
    scores = scores * score_scale
    masked = allowed[:, None, None, :]
    scores = jnp.where(masked, scores, MASKED_SCORE)
    peaks = jnp.max(scores, axis=-1)
    weights = jnp.where(masked, jnp.exp(scores - peaks[..., None]), 0.0)
    totals = jnp.sum(weights, axis=-1)
    formula = "nkgs,nskd->nkgd"
    weighted = jnp.einsum(
        formula, weights, value_block.astype(jnp.float32), precision=lax.Precision.HIGHEST
    )
    return (weighted, peaks, totals)


def merge_parts(left_part, right_part):
    peaks = jnp.maximum(left_part[1], right_part[1])
    scale_left = jnp.exp(left_part[1] - peaks)
    scale_right = jnp.exp(right_part[1] - peaks)
    weighted = left_part[0] * scale_left[..., None] + right_part[0] * scale_right[..., None]
    return (weighted, peaks, left_part[2] * scale_left + right_part[2] * scale_right)


def split_rows(rows, kv_heads_local, head_dim):
    count_rows = rows.shape[0]
    return (
        rows[:, :, 0].reshape(count_rows, -1, kv_heads_local, head_dim),
        rows[:, :, 1].reshape(count_rows, -1, kv_heads_local, head_dim),
    )


def local(queries, new_kv, own_kv, prompt_kv, out_weight, parents, own_len, first_beam):
    per_dev = queries.shape[0]
    head_dim = HD
    kv_heads_local = new_kv.shape[2] // head_dim
    q_heads_local = queries.shape[1] // head_dim
    group_size = q_heads_local // kv_heads_local
    own_size = own_kv.shape[1]
    dev_index = lax.axis_index("req")
    reach_dev = (MOST_BEAMS - 2) // per_dev + 1
    offsets = list(range(-reach_dev, reach_dev + 1))
    slot_ids = jnp.arange(per_dev, dtype=jnp.int32)
    my_beams = dev_index * per_dev + slot_ids
    own_positions = jnp.arange(own_size, dtype=jnp.int32)
    query_block = queries.reshape(per_dev, kv_heads_local, group_size, head_dim)
    fresh_keys, fresh_values = split_rows(new_kv[:, None], kv_heads_local, head_dim)
    fresh_allowed = jnp.ones((per_dev, 1), bool)
    merged = partial_block(query_block, fresh_keys, fresh_values, fresh_allowed)
    home_gap = dev_index - first_beam[my_beams] // per_dev
    prompt_list = [prompt_kv[0]]
    for offset in range(1, reach_dev + 1):
        prompt_list.append(from_behind(prompt_kv, "req", offset)[0])
    prompt_stack = jnp.stack(prompt_list)
    beam_prompt = prompt_stack[home_gap]
    pieces = []
    for offset in offsets:
        if offset == 0:
            pieces.append(own_kv)
        else:
            pieces.append(from_behind(own_kv, "req", -offset))
    stacked = jnp.concatenate(pieces, axis=0)
    parent = parents[my_beams]
    picked = (parent // per_dev - dev_index + reach_dev) * per_dev + parent % per_dev
    parent_cache = stacked[picked]
    lengths = own_len[parent]
    allowed = own_positions[None, :] < lengths[:, None]
    allowed_all = jnp.concatenate(
        [jnp.ones((per_dev, beam_prompt.shape[1]), bool), allowed], axis=1
    )
    key_rows, value_rows = split_rows(
        jnp.concatenate([beam_prompt, parent_cache], axis=1), kv_heads_local, head_dim
    )
    merged = merge_parts(merged, partial_block(query_block, key_rows, value_rows, allowed_all))
    weighted, peaks, totals = merged
    attended = (
        (weighted / totals[..., None])
        .reshape(per_dev, q_heads_local * head_dim)
        .astype(jnp.bfloat16)
    )
    partial_term = jnp.dot(attended, out_weight, preferred_element_type=jnp.float32)
    return lax.psum_scatter(
        partial_term.astype(jnp.bfloat16), "tp", scatter_dimension=1, tiled=True
    )


def solution(mesh):
    in_specs = (
        P("req", "tp"),
        P("req", None, "tp"),
        P("req", None, None, "tp"),
        P("req", None, None, "tp"),
        P("tp", None),
        P(),
        P(),
        P(),
    )
    out_specs = P("req", "tp")
    return jax.shard_map(local, mesh=mesh, in_specs=in_specs, out_specs=out_specs, check_vma=False)
```

profile of v0, /device:TPU:0, one launch (start us, length us, event | category | flops | bytes accessed | tf_op | source)
XLA Modules:
  0.0 94.9 jit_solution(3823439783219551940)
XLA Ops:
  6.6 2.0 %copy.14 = bf16[8,128,2,128]{3,1,2,0:T(8,128)(2,1)} copy(bf16[8,128,2,128]{3,2,1,0:T(2,128)(2,1)} %param.10) | data formatting | bytes 1048576 | tf_op args[2]
  8.6 4.9 %collective-permute-start.2 = (bf16[8,128,2,128]{3,1,2,0:T(8,128)(2,1)}, bf16[8,128,2,128]{3,1,2,0:T(8,128)(2,1)S(1)}, u32[]{:S(2)}, u32[]{:S(2)}) collective-permute-start(bf16[8,128,2,128]{3,1,2,0:T(8,128)(2,1)} %copy.14), channel_id=1, source_target_pairs={{0,8},{4,12},{8,16},{12,20},{16,24},{20,28},{1,9},{5,13},{9,17},{1... | collective-permute-start | bytes 1572872 | tf_op jit(solution)/shard_map/ppermute | solution.py:16
  13.5 4.2 %collective-permute-start.3 = (bf16[8,128,2,128]{3,1,2,0:T(8,128)(2,1)}, bf16[8,128,2,128]{3,1,2,0:T(8,128)(2,1)}, u32[]{:S(2)}, u32[]{:S(2)}) collective-permute-start(bf16[8,128,2,128]{3,1,2,0:T(8,128)(2,1)} %copy.14), channel_id=1, source_target_pairs={{0,4},{4,8},{8,12},{12,16},{16,20},{20,24},{24,28},{1,5},{5,9},{9,... | collective-permute-start | bytes 1572872 | tf_op jit(solution)/shard_map/ppermute | solution.py:16
  17.7 1.3 %collective-permute-start.4 = (bf16[8,128,2,128]{3,1,2,0:T(8,128)(2,1)}, bf16[8,128,2,128]{3,1,2,0:T(8,128)(2,1)}, u32[]{:S(2)}, u32[]{:S(2)}) collective-permute-start(bf16[8,128,2,128]{3,1,2,0:T(8,128)(2,1)} %copy.14), channel_id=1, source_target_pairs={{4,0},{8,4},{12,8},{16,12},{20,16},{24,20},{28,24},{5,1},{9,5},{13... | collective-permute-start | bytes 1572872 | tf_op jit(solution)/shard_map/ppermute | solution.py:16
  19.0 1.0 %copy.13 = bf16[1,512,2,128]{3,1,2,0:T(8,128)(2,1)S(1)} copy(bf16[1,512,2,128]{3,2,1,0:T(2,128)(2,1)} %param.11) | data formatting | bytes 524288 | tf_op args[3]
  20.0 4.6 %collective-permute-start = (bf16[1,512,2,128]{3,1,2,0:T(8,128)(2,1)S(1)}, bf16[1,512,2,128]{3,1,2,0:T(8,128)(2,1)S(1)}, u32[]{:S(2)}, u32[]{:S(2)}) collective-permute-start(bf16[1,512,2,128]{3,1,2,0:T(8,128)(2,1)S(1)} %copy.13), channel_id=1, source_target_pairs={{0,4},{4,8},{8,12},{12,16},{16,20},{20,24},{24,28},{1,5},{5,9},{9,... | collective-permute-start | bytes 786440 | tf_op jit(solution)/shard_map/ppermute | solution.py:16
  24.6 2.7 %collective-permute-start.1 = (bf16[1,512,2,128]{3,1,2,0:T(8,128)(2,1)S(1)}, bf16[1,512,2,128]{3,1,2,0:T(8,128)(2,1)S(1)}, u32[]{:S(2)}, u32[]{:S(2)}) collective-permute-start(bf16[1,512,2,128]{3,1,2,0:T(8,128)(2,1)S(1)} %copy.13), channel_id=1, source_target_pairs={{0,8},{4,12},{8,16},{12,20},{16,24},{20,28},{1,9},{5,13},{9,17},{1... | collective-permute-start | bytes 786440 | tf_op jit(solution)/shard_map/ppermute | solution.py:16
  27.3 0.6 gather_fusion
  28.0 1.3 %gather_fusion.2 = s32[8]{0:T(128)S(1)} fusion(s32[64]{0:T(128)} %param.15, s32[1024]{0:T(1024)S(1)} %pad_clamp_fusion.3), kind=kCustom, calls=%fused_computation.2 | custom fusion | bytes 96 | tf_op jit(solution)/shard_map/gather | solution.py:70
  29.3 0.6 gather_fusion.1
  30.2 14.7 %collective-permute-done = bf16[1,512,2,128]{3,1,2,0:T(8,128)(2,1)S(1)} collective-permute-done((bf16[1,512,2,128]{3,1,2,0:T(8,128)(2,1)S(1)}, bf16[1,512,2,128]{3,1,2,0:T(8,128)(2,1)S(1)}, u32[]{:S(2)}, u32[]{:S(2)}) %collective-permute-start) | collective-permute-done | bytes 262176 | tf_op jit(solution)/shard_map/ppermute | solution.py:16
  44.9 1.3 %collective-permute-start.5 = (bf16[8,128,2,128]{3,1,2,0:T(8,128)(2,1)}, bf16[8,128,2,128]{3,1,2,0:T(8,128)(2,1)}, u32[]{:S(2)}, u32[]{:S(2)}) collective-permute-start(bf16[8,128,2,128]{3,1,2,0:T(8,128)(2,1)} %copy.14), channel_id=1, source_target_pairs={{8,0},{12,4},{16,8},{20,12},{24,16},{28,20},{9,1},{13,5},{17,9},{2... | collective-permute-start | bytes 1572872 | tf_op jit(solution)/shard_map/ppermute | solution.py:16
  46.3 1.0 %gather_fusion.3 = bf16[8,512,2,128]{3,1,2,0:T(8,128)(2,1)S(1)} fusion(bf16[3,512,2,128]{3,1,2,0:T(8,128)(2,1)S(1)} %pad_maximum_fusion, s32[1024]{0:T(1024)S(1)} %pad_clamp_fusion.1), kind=kCustom, calls=%fused_computation.3 | custom fusion | bytes 4194336 | tf_op jit(solution)/shard_map/gather | solution.py:75
  47.2 1.7 %constant_dynamic-update-slice_fusion.6 = bf16[8,640,2,128]{3,1,2,0:T(8,128)(2,1)} fusion(bf16[8,512,2,128]{3,1,2,0:T(8,128)(2,1)S(1)} %gather_fusion.3), kind=kLoop, calls=%fused_computation.35 | loop fusion | bytes 4194304
  49.0 0.8 constant_dynamic-update-slice_fusion.4
  49.8 2.1 %constant_dynamic-update-slice_fusion.3 = bf16[40,128,2,128]{3,1,2,0:T(8,128)(2,1)} fusion(bf16[40,128,2,128]{3,1,2,0:T(8,128)(2,1)} %constant_dynamic-update-slice_fusion.4, bf16[8,128,2,128]{3,1,2,0:T(8,128)(2,1)} %collective-permute-done.3), kind=kLoop, calls=%fused_computation.32 | loop fusion | bytes 1048576
  51.9 0.9 constant_dynamic-update-slice_fusion.2
  52.8 1.9 %constant_dynamic-update-slice_fusion.1 = bf16[40,128,2,128]{3,1,2,0:T(8,128)(2,1)} fusion(bf16[40,128,2,128]{3,1,2,0:T(8,128)(2,1)} %constant_dynamic-update-slice_fusion.2, bf16[8,128,2,128]{3,1,2,0:T(8,128)(2,1)} %collective-permute-done.4), kind=kLoop, calls=%fused_computation.30 | loop fusion | bytes 1048576
  54.7 4.9 %collective-permute-done.5 = bf16[8,128,2,128]{3,1,2,0:T(8,128)(2,1)} collective-permute-done((bf16[8,128,2,128]{3,1,2,0:T(8,128)(2,1)}, bf16[8,128,2,128]{3,1,2,0:T(8,128)(2,1)}, u32[]{:S(2)}, u32[]{:S(2)}) %collective-permute-start.5) | collective-permute-done | bytes 524320 | tf_op jit(solution)/shard_map/ppermute | solution.py:16
  59.6 1.9 %constant_dynamic-update-slice_fusion = bf16[40,128,2,128]{3,1,2,0:T(8,128)(2,1)} fusion(bf16[40,128,2,128]{3,1,2,0:T(8,128)(2,1)} %constant_dynamic-update-slice_fusion.1, bf16[8,128,2,128]{3,1,2,0:T(8,128)(2,1)} %collective-permute-done.5), kind=kLoop, calls=%fused_computation.29 | loop fusion | bytes 1048576 | tf_op jit(solution)/shard_map/concatenate | solution.py:82
  61.4 2.4 %gather_fusion.4 = bf16[8,128,2,128]{3,1,2,0:T(8,128)(2,1)S(1)} fusion(bf16[40,128,2,128]{3,1,2,0:T(8,128)(2,1)} %constant_dynamic-update-slice_fusion, s32[1024]{0:T(1024)S(1)} %pad_clamp_fusion), kind=kCustom, calls=%fused_computation.4 | custom fusion | bytes 1048608 | tf_op jit(solution)/shard_map/gather | solution.py:85
  64.7 0.8 fusion.9
  66.0 1.3 %convolution_convert_fusion = bf16[8,2048]{1,0:T(8,128)(2,1)} fusion(bf16[1024,2048]{1,0:T(8,128)(2,1)S(1)} %copy-done.2, bf16[1,8,8,128]{3,2,1,0:T(8,128)(2,1)S(1)} %fusion.9), kind=kOutput, calls=%fused_computation.5 | convolution fusion | flops 33570816 | bytes 4243456 | tf_op jit(solution)/shard_map/dot_general | solution.py:101
  67.3 20.7 %reduce-scatter.2.cloned.1.call-done = bf16[8,512]{1,0:T(8,128)(2,1)} async-done(((bf16[8,2048]{1,0:T(8,128)(2,1)}), bf16[8,512]{1,0:T(8,128)(2,1)}) %reduce-scatter.2.cloned.1.call-update) | async-done | bytes 8208 | tf_op jit(solution)/shard_map/reduce_scatter | solution.py:102
  (37 shorter events, 1.8 us)
Async XLA Ops:
  6.5 20.8 %copy-start = (s32[64]{0:T(128)S(1)}, s32[64]{0:T(128)}, u32[]{:S(2)}) copy-start(s32[64]{0:T(128)} %param.13) | copy-start | bytes 772
  6.5 22.7 %copy-start.1 = (s32[64]{0:T(128)S(1)}, s32[64]{0:T(128)}, u32[]{:S(2)}) copy-start(s32[64]{0:T(128)} %param.14) | copy-start | bytes 772
  6.5 23.5 %copy-start.5 = (bf16[8,2,128]{2,1,0:T(2,128)(2,1)S(1)}, bf16[8,2,128]{2,1,0:T(2,128)(2,1)}, u32[]{:S(2)}) copy-start(bf16[8,2,128]{2,1,0:T(2,128)(2,1)} %param.9) | copy-start | bytes 12292
  6.5 23.5 %copy-start.6 = (bf16[8,1024]{1,0:T(8,128)(2,1)S(1)}, bf16[8,1024]{1,0:T(8,128)(2,1)}, u32[]{:S(2)}) copy-start(bf16[8,1024]{1,0:T(8,128)(2,1)} %param.8) | copy-start | bytes 49156
  6.5 81.5 %reduce-scatter.2.cloned.1.call-start = ((), (), s32[]{:S(2)}) async-start(), calls=%async_computation.1 | async-start | bytes 40960 | tf_op jit(solution)/shard_map/reduce_scatter | solution.py:102
  8.6 40.4 %collective-permute-start.2 = (bf16[8,128,2,128]{3,1,2,0:T(8,128)(2,1)}, bf16[8,128,2,128]{3,1,2,0:T(8,128)(2,1)S(1)}, u32[]{:S(2)}, u32[]{:S(2)}) collective-permute-start(bf16[8,128,2,128]{3,1,2,0:T(8,128)(2,1)} %copy.14), channel_id=1, source_target_pairs={{0,8},{4,12},{8,16},{12,20},{16,24},{20,28},{1,9},{5,13},{9,17},{1... | collective-permute-start | bytes 1572872 | tf_op jit(solution)/shard_map/ppermute | solution.py:16
  13.5 36.3 %collective-permute-start.3 = (bf16[8,128,2,128]{3,1,2,0:T(8,128)(2,1)}, bf16[8,128,2,128]{3,1,2,0:T(8,128)(2,1)}, u32[]{:S(2)}, u32[]{:S(2)}) collective-permute-start(bf16[8,128,2,128]{3,1,2,0:T(8,128)(2,1)} %copy.14), channel_id=1, source_target_pairs={{0,4},{4,8},{8,12},{12,16},{16,20},{20,24},{24,28},{1,5},{5,9},{9,... | collective-permute-start | bytes 1572872 | tf_op jit(solution)/shard_map/ppermute | solution.py:16
  17.7 35.0 %collective-permute-start.4 = (bf16[8,128,2,128]{3,1,2,0:T(8,128)(2,1)}, bf16[8,128,2,128]{3,1,2,0:T(8,128)(2,1)}, u32[]{:S(2)}, u32[]{:S(2)}) collective-permute-start(bf16[8,128,2,128]{3,1,2,0:T(8,128)(2,1)} %copy.14), channel_id=1, source_target_pairs={{4,0},{8,4},{12,8},{16,12},{20,16},{24,20},{28,24},{5,1},{9,5},{13... | collective-permute-start | bytes 1572872 | tf_op jit(solution)/shard_map/ppermute | solution.py:16
  20.0 24.9 %collective-permute-start = (bf16[1,512,2,128]{3,1,2,0:T(8,128)(2,1)S(1)}, bf16[1,512,2,128]{3,1,2,0:T(8,128)(2,1)S(1)}, u32[]{:S(2)}, u32[]{:S(2)}) collective-permute-start(bf16[1,512,2,128]{3,1,2,0:T(8,128)(2,1)S(1)} %copy.13), channel_id=1, source_target_pairs={{0,4},{4,8},{8,12},{12,16},{16,20},{20,24},{24,28},{1,5},{5,9},{9,... | collective-permute-start | bytes 786440 | tf_op jit(solution)/shard_map/ppermute | solution.py:16
  24.6 21.6 %collective-permute-start.1 = (bf16[1,512,2,128]{3,1,2,0:T(8,128)(2,1)S(1)}, bf16[1,512,2,128]{3,1,2,0:T(8,128)(2,1)S(1)}, u32[]{:S(2)}, u32[]{:S(2)}) collective-permute-start(bf16[1,512,2,128]{3,1,2,0:T(8,128)(2,1)S(1)} %copy.13), channel_id=1, source_target_pairs={{0,8},{4,12},{8,16},{12,20},{16,24},{20,28},{1,9},{5,13},{9,17},{1... | collective-permute-start | bytes 786440 | tf_op jit(solution)/shard_map/ppermute | solution.py:16
  44.9 14.7 %collective-permute-start.5 = (bf16[8,128,2,128]{3,1,2,0:T(8,128)(2,1)}, bf16[8,128,2,128]{3,1,2,0:T(8,128)(2,1)}, u32[]{:S(2)}, u32[]{:S(2)}) collective-permute-start(bf16[8,128,2,128]{3,1,2,0:T(8,128)(2,1)} %copy.14), channel_id=1, source_target_pairs={{8,0},{12,4},{16,8},{20,12},{24,16},{28,20},{9,1},{13,5},{17,9},{2... | collective-permute-start | bytes 1572872 | tf_op jit(solution)/shard_map/ppermute | solution.py:16
  47.2 4.6 %copy-start.3 = (bf16[8,128,2,128]{3,2,1,0:T(2,128)(2,1)S(1)}, bf16[8,128,2,128]{3,2,1,0:T(2,128)(2,1)}, u32[]{:S(2)}) copy-start(bf16[8,128,2,128]{3,2,1,0:T(2,128)(2,1)} %param.10) | copy-start | bytes 1572868
  49.8 14.0 %copy-start.4 = (bf16[8,640,2,128]{3,1,2,0:T(8,128)(2,1)S(1)}, bf16[8,640,2,128]{3,1,2,0:T(8,128)(2,1)}, u32[]{:S(2)}) copy-start(bf16[8,640,2,128]{3,1,2,0:T(8,128)(2,1)} %constant_dynamic-update-slice_fusion.6) | copy-start | bytes 7864324
  63.8 2.2 %copy-start.2 = (bf16[1024,2048]{1,0:T(8,128)(2,1)S(1)}, bf16[1024,2048]{1,0:T(8,128)(2,1)}, u32[]{:S(2)}) copy-start(bf16[1024,2048]{1,0:T(8,128)(2,1)} %param.12) | copy-start | bytes 12582916
Sparse Core Ops, SparseCore 0:
  67.4 20.5 reduce-scatter.1
where the time goes:
time: 95.3 us; the launch traced here: 94.9 us
  waiting for transfers between devices  40.3 us (42%)
  starting transfers between devices  19 us (20%)
  local copies, waits for them, and re-layouts  18.8 us (20%)
  between operations  13.6 us (14%)
  matrix products  2.76 us (3%)
    reduce_scatter x1, waiting for transfers between devices, local(): lax.psum_scatter(partial_term.astype(jnp.bfloat16), 'tp', scatter_dimensi...  20.7 us
    ppermute x6, waiting for transfers between devices, from_behind(): return lax.ppermute(block, axis, route)  19.6 us
    ppermute x6, starting transfers between devices, from_behind(): return lax.ppermute(block, axis, route)  18.9 us
    unnamed x22, local copies, waits for them, and re-layouts  10.9 us
    gather x1, local copies, waits for them, and re-layouts, local(): parent_cache = stacked[picked]  2.39 us
  transfers between devices with their start and end apart: 7, of which 3 were waited for; matrix products, arithmetic and copies ran while one was open for 13% of the time, Pallas kernels for 0%

commit v1 on v0

v1 whole, which is shorter than its diff:
```python
import functools

import jax
import jax.numpy as jnp
from jax import lax
from jax.experimental import pallas as pl
from jax.experimental.pallas import tpu as pltpu
from jax.sharding import PartitionSpec as P

HD = 128
MOST_BEAMS = 16
NEG = -1e30
MESH = pl.DeviceIdType.MESH

NEAR = (1, 2, -1, -2)


def nt(a, b):
    return lax.dot_general(
        a, b, (((1,), (1,)), ((), ())), preferred_element_type=jnp.float32
    )


def kernel(
    n, n_tp,
    q_ref, new_ref, own_hbm, prompt_hbm, w_hbm, parents, own_len, first_beam,
    out_ref,
    qs, qin, kvb, kvf, newf, kb, vb, wv, res, rin, part, pin,
    load_sem, q_send, q_recv, r_send, r_recv, o_send, o_recv,
):
    per_dev = q_ref.shape[0]
    groups = q_ref.shape[1] // HD
    rows = per_dev * groups
    own_rows, prompt_rows = own_hbm.shape[0], prompt_hbm.shape[0]
    n_own, n_prompt = own_rows // 2, prompt_rows // 2
    n_keys = n_own + n_prompt
    cache = n_own // per_dev
    scale = HD ** -0.5
    d = lax.axis_index("req")
    t = lax.axis_index("tp")

    def there(delta):
        return d + delta < n if delta > 0 else d + delta >= 0

    own_load = pltpu.make_async_copy(own_hbm, kvb.at[pl.ds(0, own_rows)], load_sem.at[0])
    prompt_load = pltpu.make_async_copy(
        prompt_hbm, kvb.at[pl.ds(own_rows, prompt_rows)], load_sem.at[1]
    )
    w_load = pltpu.make_async_copy(w_hbm, wv, load_sem.at[2])

    barrier = pltpu.get_barrier_semaphore()
    for delta in NEAR:
        @pl.when(there(delta))
        def _():
            pl.semaphore_signal(
                barrier, inc=1, device_id={"req": d + delta}, device_id_type=MESH
            )
    for j in range(1, n_tp):
        pl.semaphore_signal(
            barrier, inc=1, device_id={"tp": lax.rem(t + j, n_tp)}, device_id_type=MESH
        )
    own_load.start()
    prompt_load.start()
    w_load.start()

    qf = q_ref[...].astype(jnp.float32)
    qrows = jnp.concatenate([qf[:, g * HD:(g + 1) * HD] for g in range(groups)], axis=0)
    qs[...] = qrows.astype(jnp.bfloat16)

    for k, delta in enumerate(NEAR):
        @pl.when(jnp.logical_not(there(delta)))
        def _():
            qin[pl.ds(k * rows, rows), :] = jnp.zeros((rows, HD), jnp.bfloat16)
            rin[k] = jnp.zeros(rin.shape[1:], jnp.bfloat16)

    peers = n_tp - 1
    for delta in NEAR:
        peers = peers + jnp.where(there(delta), 1, 0)
    pl.semaphore_wait(barrier, peers)

    def q_copy(k, target):
        return pltpu.make_async_remote_copy(
            src_ref=qs,
            dst_ref=qin.at[pl.ds(k * rows, rows)],
            send_sem=q_send.at[k],
            recv_sem=q_recv.at[k],
            device_id={"req": target},
            device_id_type=MESH,
        )

    def r_copy(k_from, k_to, target):
        return pltpu.make_async_remote_copy(
            src_ref=res.at[k_from],
            dst_ref=rin.at[k_to],
            send_sem=r_send.at[k_to],
            recv_sem=r_recv.at[k_to],
            device_id={"req": target},
            device_id_type=MESH,
        )

    for delta in NEAR:
        @pl.when(there(delta))
        def _():
            q_copy(NEAR.index(-delta), d + delta).start()

    sub = lax.broadcasted_iota(jnp.int32, (per_dev, HD), 0)
    lane = lax.broadcasted_iota(jnp.int32, (per_dev, HD), 1)

    def beam_facts(delta):
        source = lax.rem(d + delta + n, n)
        rel = jnp.zeros((per_dev, HD), jnp.int32)
        length = jnp.zeros((per_dev, HD), jnp.int32)
        gap = jnp.zeros((per_dev, HD), jnp.int32)
        for i in range(per_dev):
            b = source * per_dev + i
            parent = parents[b]
            here = sub == i
            rel = jnp.where(here, parent - d * per_dev, rel)
            length = jnp.where(here, own_len[parent], length)
            if delta >= 0:
                gap = jnp.where(here, first_beam[b] - d * per_dev, gap)
        return rel, length, gap

    facts = {delta: beam_facts(delta) for delta in (0,) + NEAR}

    def spread(deltas, which):
        return jnp.concatenate(
            [facts[delta][which] for delta in deltas for _ in range(groups)], axis=0
        )

    newf[...] = new_ref[...].astype(jnp.float32)
    new_k = newf[pl.ds(0, per_dev, stride=2), :]
    new_v = newf[pl.ds(1, per_dev, stride=2), :]

    own_load.wait()
    kvf[pl.ds(0, own_rows), :] = kvb[pl.ds(0, own_rows), :].astype(jnp.float32)
    prompt_load.wait()
    kvf[pl.ds(own_rows, prompt_rows), :] = kvb[pl.ds(own_rows, prompt_rows), :].astype(jnp.float32)
    kb[...] = kvf[pl.ds(0, n_keys, stride=2), :].astype(jnp.bfloat16)
    vb[...] = kvf[pl.ds(1, n_keys, stride=2), :].astype(jnp.bfloat16)

    def attend(q, deltas, fresh=None):
        rel = spread(deltas, 0)
        length = spread(deltas, 1)
        lanes = lax.broadcasted_iota(jnp.int32, rel.shape, 1)
        s = jnp.full(rel.shape, NEG, jnp.float32)
        for c in range(per_dev):
            s = jnp.where(rel == c, nt(q, kb[pl.ds(c * cache, cache), :]), s)
        s = jnp.where(lanes < length, s, NEG)
        prompt = []
        if min(deltas) >= 0:
            gap = spread(deltas, 2)
            mine = (gap >= 0) & (gap < per_dev)
            for c in range(n_prompt // HD):
                sp = nt(q, kb[pl.ds(n_own + c * HD, HD), :])
                prompt.append(jnp.where(mine, sp, NEG))
        top = functools.reduce(jnp.maximum, prompt, s)
        m = jnp.max(top, axis=1, keepdims=True)
        if fresh is not None:
            m = jnp.maximum(m, fresh)
        p = jnp.exp((s - m) * scale)
        weights = [jnp.exp((sp - m) * scale).astype(jnp.bfloat16) for sp in prompt]
        total = functools.reduce(
            jnp.add,
            [x.astype(jnp.float32) for x in weights],
            p.astype(jnp.bfloat16).astype(jnp.float32),
        )
        total = jnp.sum(total, axis=1, keepdims=True)
        picked = [jnp.where(rel == c, p, 0.0).astype(jnp.bfloat16) for c in range(per_dev)]
        table = jnp.concatenate(picked + weights, axis=1)
        w = jnp.dot(table, vb[pl.ds(0, table.shape[1]), :], preferred_element_type=jnp.float32)
        return m, total, w

    k_tiled = jnp.concatenate([new_k] * groups, axis=0)
    v_tiled = jnp.concatenate([new_v] * groups, axis=0)
    fresh = jnp.sum(qrows * k_tiled, axis=1, keepdims=True)
    m0, l0, w0 = attend(qs[...], (0,), fresh)
    pf = jnp.exp((fresh - m0) * scale)
    l0 = l0 + pf
    w0 = w0 + pf * v_tiled

    for pair in (0, 1):
        deltas = NEAR[2 * pair:2 * pair + 2]
        for k in (2 * pair, 2 * pair + 1):
            @pl.when(there(NEAR[k]))
            def _():
                q_copy(k, d + NEAR[k]).wait_recv()
        m, total, w = attend(qin[pl.ds(2 * pair * rows, 2 * rows), :], deltas)
        lanes = lax.broadcasted_iota(jnp.int32, w.shape, 1)
        stats = jnp.zeros(w.shape, jnp.float32)
        at = 0
        for value, count in ((m, 3), (total, 2)):
            left = value
            for _ in range(count):
                piece = left.astype(jnp.bfloat16).astype(jnp.float32)
                left = left - piece
                stats = jnp.where(lanes == at, piece, stats)
                at += 1
        for i in (0, 1):
            k = 2 * pair + i
            res[k, :, pl.ds(0, HD)] = w[i * rows:(i + 1) * rows].astype(jnp.bfloat16)
            res[k, :, pl.ds(HD, HD)] = stats[i * rows:(i + 1) * rows].astype(jnp.bfloat16)
            @pl.when(there(NEAR[k]))
            def _():
                r_copy(k, NEAR.index(-NEAR[k]), d + NEAR[k]).start()

    parts = [(m0, l0, w0)]
    for k, delta in enumerate(NEAR):
        @pl.when(there(delta))
        def _():
            r_copy(k, k, d + delta).wait_recv()
        w = rin[k, :, pl.ds(0, HD)].astype(jnp.float32)
        st = rin[k, :, pl.ds(HD, HD)].astype(jnp.float32)
        m = st[:, 0:1] + st[:, 1:2] + st[:, 2:3]
        l = st[:, 3:4] + st[:, 4:5]
        m = jnp.where(there(delta), m, NEG)
        parts.append((m, l, w))
    peak = functools.reduce(jnp.maximum, [x[0] for x in parts])
    weighted = jnp.zeros((rows, HD), jnp.float32)
    total = jnp.zeros((rows, 1), jnp.float32)
    for m, l, w in parts:
        f = jnp.exp((m - peak) * scale)
        weighted = weighted + w * f
        total = total + l * f
    att = weighted / total
    att = jnp.concatenate(
        [att[g * per_dev:(g + 1) * per_dev] for g in range(groups)], axis=1
    ).astype(jnp.bfloat16)

    w_load.wait()
    width = w_hbm.shape[1] // n_tp

    def o_copy(j):
        return pltpu.make_async_remote_copy(
            src_ref=part.at[j - 1],
            dst_ref=pin.at[j - 1],
            send_sem=o_send.at[j - 1],
            recv_sem=o_recv.at[j - 1],
            device_id={"tp": lax.rem(t + j, n_tp)},
            device_id_type=MESH,
        )

    def project(j):
        start = pl.multiple_of(lax.rem(t + j, n_tp) * width, width)
        y = jnp.dot(att, wv[:, pl.ds(start, width)], preferred_element_type=jnp.float32)
        return jnp.concatenate([y[:, :width // 2], y[:, width // 2:]], axis=0)

    for j in range(n_tp - 1, 0, -1):
        part[j - 1] = project(j).astype(jnp.bfloat16)
        o_copy(j).start()
    y = project(0)
    for j in range(n_tp - 1, 0, -1):
        o_copy(j).wait_recv()
        y = y + pin[j - 1].astype(jnp.float32)
    y = jnp.concatenate([y[:per_dev], y[per_dev:]], axis=1)
    out_ref[...] = y.astype(jnp.bfloat16)

    for k, delta in enumerate(NEAR):
        @pl.when(there(delta))
        def _():
            q_copy(NEAR.index(-delta), d + delta).wait_send()
            r_copy(k, NEAR.index(-delta), d + delta).wait_send()
    for j in range(1, n_tp):
        o_copy(j).wait_send()


def local(n, n_tp, queries, new_kv, own_kv, prompt_kv, out_weight, parents, own_len, first_beam):
    per_dev, q_width = queries.shape
    rows = per_dev * q_width // HD
    own = own_kv.reshape(-1, HD)
    prompt = prompt_kv.reshape(-1, HD)
    new = new_kv.reshape(-1, HD)
    total = own.shape[0] + prompt.shape[0]
    width = out_weight.shape[1] // n_tp
    vmem = pl.BlockSpec(memory_space=pltpu.VMEM)
    smem = pl.BlockSpec(memory_space=pltpu.SMEM)
    hbm = pl.BlockSpec(memory_space=pl.ANY)
    near = len(NEAR)
    bf16, f32 = jnp.bfloat16, jnp.float32
    dma = pltpu.SemaphoreType.DMA
    return pl.pallas_call(
        functools.partial(kernel, n, n_tp),
        out_shape=jax.ShapeDtypeStruct((per_dev, width), bf16),
        in_specs=[vmem, vmem, hbm, hbm, hbm, smem, smem, smem],
        out_specs=vmem,
        scratch_shapes=[
            pltpu.VMEM((rows, HD), bf16),
            pltpu.VMEM((near * rows, HD), bf16),
            pltpu.VMEM((total, HD), bf16),
            pltpu.VMEM((total, HD), f32),
            pltpu.VMEM(new.shape, f32),
            pltpu.VMEM((total // 2, HD), bf16),
            pltpu.VMEM((total // 2, HD), bf16),
            pltpu.VMEM(out_weight.shape, bf16),
            pltpu.VMEM((near, rows, 2 * HD), bf16),
            pltpu.VMEM((near, rows, 2 * HD), bf16),
            pltpu.VMEM((n_tp - 1, 2 * per_dev, width // 2), bf16),
            pltpu.VMEM((n_tp - 1, 2 * per_dev, width // 2), bf16),
            dma((3,)),
            dma((near,)),
            dma((near,)),
            dma((near,)),
            dma((near,)),
            dma((n_tp - 1,)),
            dma((n_tp - 1,)),
        ],
        compiler_params=pltpu.CompilerParams(
            collective_id=0, has_side_effects=True, vmem_limit_bytes=48 * 1024 * 1024
        ),
    )(queries, new, own, prompt, out_weight, parents, own_len, first_beam)


def solution(mesh):
    in_specs = (
        P("req", "tp"),
        P("req", None, "tp"),
        P("req", None, None, "tp"),
        P("req", None, None, "tp"),
        P("tp", None),
        P(),
        P(),
        P(),
    )
    out_specs = P("req", "tp")
    run = functools.partial(local, mesh.shape["req"], mesh.shape["tp"])
    return jax.shard_map(run, mesh=mesh, in_specs=in_specs, out_specs=out_specs, check_vma=False)
```

time: 95.3 us -> 25.1 us (0.26)
  waiting for transfers between devices: 40.3 us -> 0 us
  starting transfers between devices: 19 us -> 0 us
  Pallas kernels: 0 us -> 16.6 us
  between operations: 13.6 us -> 0.02 us
  local copies, waits for them, and re-layouts: 18.8 us -> 8.15 us
  matrix products: 2.76 us -> 0 us
    reduce_scatter x1 -> x0, waiting for transfers between devices: 20.7 us -> none  [local(): lax.psum_scatter(partial_term.astype(jnp.bfloat16), 'tp', scatter_dimensi...]
    ppermute x6 -> x0, waiting for transfers between devices: 19.6 us -> none  [from_behind(): return lax.ppermute(block, axis, route)]
    ppermute x6 -> x0, starting transfers between devices: 18.9 us -> none  [from_behind(): return lax.ppermute(block, axis, route)]
    pallas_call x0 -> x1, Pallas kernels: none -> 16.6 us  [local(): pl.pallas_call(functools.partial(kernel, n, n_tp), out_shape=jax.ShapeDty...]
    gather x5 -> x0, local copies, waits for them, and re-layouts: 5.92 us -> none  [the longest x1 2.39 us: local(): parent_cache = stacked[picked]]
    unnamed x22 -> x17, local copies, waits for them, and re-layouts: 10.9 us -> 8.15 us
    dot_general x4 -> x0, matrix products: 2.76 us -> none  [the longest x1 1.26 us: local(): jnp.dot(attended, out_weight, preferred_element_type=jnp.float32)]
    concatenate x3 -> x0, local copies, waits for them, and re-layouts: 1.96 us -> none  [the longest x1 1.89 us: local(): stacked = jnp.concatenate(pieces, axis=0)]
  transfers between devices with their start and end apart: 7 -> 0, of which waited for: 3 -> 0; matrix products, arithmetic and copies ran while one was open for 13% -> 0% of each run, Pallas kernels for 0% -> 0%
where the time goes in v1:
time: 25.1 us; the launch traced here: 24.7 us
  Pallas kernels  16.6 us (66%)
  local copies, waits for them, and re-layouts  8.15 us (32%)
    pallas_call x1, Pallas kernels, local(): pl.pallas_call(functools.partial(kernel, n, n_tp), out_shape=jax.ShapeDty...  16.6 us
    unnamed x17, local copies, waits for them, and re-layouts  8.15 us

profile of v1, /device:TPU:0, one launch (start us, length us, event | category | flops | bytes accessed | tf_op | source)
XLA Modules:
  0.0 24.7 jit_solution(6430146053960809292)
XLA Ops:
  0.0 0.0 copy-start
  0.0 2.2 %copy-done = bf16[1024,2048]{1,0:T(8,128)(2,1)S(1)} copy-done((bf16[1024,2048]{1,0:T(8,128)(2,1)S(1)}, bf16[1024,2048]{1,0:T(8,128)(2,1)}, u32[]{:S(2)}) %copy-start) | copy-done | bytes 4194328
  2.2 0.0 copy-start.1
  2.2 1.0 %copy-done.1 = bf16[8,128,2,128]{3,2,1,0:T(2,128)(2,1)S(1)} copy-done((bf16[8,128,2,128]{3,2,1,0:T(2,128)(2,1)S(1)}, bf16[8,128,2,128]{3,2,1,0:T(2,128)(2,1)}, u32[]{:S(2)}) %copy-start.1) | copy-done | bytes 524312
  3.2 0.0 copy-start.2
  3.2 0.9 %copy-done.2 = bf16[1,512,2,128]{3,2,1,0:T(2,128)(2,1)S(1)} copy-done((bf16[1,512,2,128]{3,2,1,0:T(2,128)(2,1)S(1)}, bf16[1,512,2,128]{3,2,1,0:T(2,128)(2,1)}, u32[]{:S(2)}) %copy-start.2) | copy-done | bytes 262168
  4.2 0.0 copy-start.3
  4.2 0.7 %copy-done.3 = bf16[8,1024]{1,0:T(8,128)(2,1)S(1)} copy-done((bf16[8,1024]{1,0:T(8,128)(2,1)S(1)}, bf16[8,1024]{1,0:T(8,128)(2,1)}, u32[]{:S(2)}) %copy-start.3) | copy-done | bytes 16408
  4.9 0.0 copy-start.4
  4.9 0.7 %copy-done.4 = bf16[8,2,128]{2,1,0:T(2,128)(2,1)S(1)} copy-done((bf16[8,2,128]{2,1,0:T(2,128)(2,1)S(1)}, bf16[8,2,128]{2,1,0:T(2,128)(2,1)}, u32[]{:S(2)}) %copy-start.4) | copy-done | bytes 4120
  5.6 0.0 copy-start.5
  5.6 0.7 %copy-done.5 = s32[64]{0:T(128)S(1)} copy-done((s32[64]{0:T(128)S(1)}, s32[64]{0:T(128)}, u32[]{:S(2)}) %copy-start.5) | copy-done | bytes 280
  6.2 0.0 copy-start.6
  6.2 0.7 %copy-done.6 = s32[64]{0:T(128)S(1)} copy-done((s32[64]{0:T(128)S(1)}, s32[64]{0:T(128)}, u32[]{:S(2)}) %copy-start.6) | copy-done | bytes 280
  6.9 0.0 copy-start.7
  6.9 0.7 %copy-done.7 = s32[64]{0:T(128)S(1)} copy-done((s32[64]{0:T(128)S(1)}, s32[64]{0:T(128)}, u32[]{:S(2)}) %copy-start.7) | copy-done | bytes 280
  7.6 16.6 %shard_map.82 = bf16[8,512]{1,0:T(8,128)(2,1)S(1)} custom-call(bf16[8,1024]{1,0:T(8,128)(2,1)S(1)} %copy-done.3, bf16[16,128]{1,0:T(8,128)(2,1)S(1)} %bitcast.5, bf16[2048,128]{1,0:T(8,128)(2,1)S(1)} %bitcast.3, bf16[1024,128]{1,0:T(8,128)(2,1)S(1)} %bitcast.4, bf16[1024,2048]{1,0:T(8,128)(2,1)S(1)} %copy-done, s32[64]{0:T(128)S(1)} %copy-done.5, ...), custom_call_target="tpu_custom_call" | custom-call | tf_op jit(solution)/shard_map/pallas_call | solution.py:281
  24.1 0.6 %copy.10 = bf16[8,512]{1,0:T(8,128)(2,1)} copy(bf16[8,512]{1,0:T(8,128)(2,1)S(1)} %shard_map.82) | data formatting | bytes 16384
Async XLA Ops:
  0.0 2.2 %copy-start = (bf16[1024,2048]{1,0:T(8,128)(2,1)S(1)}, bf16[1024,2048]{1,0:T(8,128)(2,1)}, u32[]{:S(2)}) copy-start(bf16[1024,2048]{1,0:T(8,128)(2,1)} %w_hbm.1) | copy-start | bytes 12582916
  2.2 1.0 %copy-start.1 = (bf16[8,128,2,128]{3,2,1,0:T(2,128)(2,1)S(1)}, bf16[8,128,2,128]{3,2,1,0:T(2,128)(2,1)}, u32[]{:S(2)}) copy-start(bf16[8,128,2,128]{3,2,1,0:T(2,128)(2,1)} %param.10) | copy-start | bytes 1572868
  3.2 0.9 %copy-start.2 = (bf16[1,512,2,128]{3,2,1,0:T(2,128)(2,1)S(1)}, bf16[1,512,2,128]{3,2,1,0:T(2,128)(2,1)}, u32[]{:S(2)}) copy-start(bf16[1,512,2,128]{3,2,1,0:T(2,128)(2,1)} %param.11) | copy-start | bytes 786436
  4.2 0.7 %copy-start.3 = (bf16[8,1024]{1,0:T(8,128)(2,1)S(1)}, bf16[8,1024]{1,0:T(8,128)(2,1)}, u32[]{:S(2)}) copy-start(bf16[8,1024]{1,0:T(8,128)(2,1)} %q_ref.1) | copy-start | bytes 49156
  4.9 0.7 %copy-start.4 = (bf16[8,2,128]{2,1,0:T(2,128)(2,1)S(1)}, bf16[8,2,128]{2,1,0:T(2,128)(2,1)}, u32[]{:S(2)}) copy-start(bf16[8,2,128]{2,1,0:T(2,128)(2,1)} %param.9) | copy-start | bytes 12292
  5.6 0.7 %copy-start.5 = (s32[64]{0:T(128)S(1)}, s32[64]{0:T(128)}, u32[]{:S(2)}) copy-start(s32[64]{0:T(128)} %parents.1) | copy-start | bytes 772
  6.2 0.7 %copy-start.6 = (s32[64]{0:T(128)S(1)}, s32[64]{0:T(128)}, u32[]{:S(2)}) copy-start(s32[64]{0:T(128)} %own_len.1) | copy-start | bytes 772
  6.9 0.7 %copy-start.7 = (s32[64]{0:T(128)S(1)}, s32[64]{0:T(128)}, u32[]{:S(2)}) copy-start(s32[64]{0:T(128)} %first_beam.1) | copy-start | bytes 772

commit v2 on v1

--- a/solution.py
+++ b/solution.py
@@ -305,7 +305,7 @@
             dma((n_tp - 1,)),
         ],
         compiler_params=pltpu.CompilerParams(
-            collective_id=0, has_side_effects=True, vmem_limit_bytes=48 * 1024 * 1024
+            collective_id=0, has_side_effects=True, vmem_limit_bytes=58 * 1024 * 1024
         ),
     )(queries, new, own, prompt, out_weight, parents, own_len, first_beam)
 

time: 25.1 us -> 18.9 us (0.75)
  local copies, waits for them, and re-layouts: 8.15 us -> 1.3 us
  Pallas kernels: 16.6 us -> 17.4 us
    unnamed x17 -> x1, local copies, waits for them, and re-layouts: 8.15 us -> 1.3 us
    pallas_call x1, Pallas kernels: 16.6 us -> 17.4 us  [local(): pl.pallas_call(functools.partial(kernel, n, n_tp), out_shape=jax.ShapeDty...]
where the time goes in v2:
time: 18.9 us; the launch traced here: 18.7 us
  Pallas kernels  17.4 us (92%)
  local copies, waits for them, and re-layouts  1.3 us (7%)
    pallas_call x1, Pallas kernels, local(): pl.pallas_call(functools.partial(kernel, n, n_tp), out_shape=jax.ShapeDty...  17.4 us
    unnamed x1, local copies, waits for them, and re-layouts  1.3 us

profile of v2, /device:TPU:0, one launch (start us, length us, event | category | flops | bytes accessed | tf_op | source)
XLA Modules:
  0.0 18.7 jit_solution(9725559379864966070)
XLA Ops:
  0.0 17.4 %shard_map.82 = bf16[8,512]{1,0:T(8,128)(2,1)} custom-call(bf16[8,1024]{1,0:T(8,128)(2,1)} %q_ref.1, bf16[16,128]{1,0:T(8,128)(2,1)} %bitcast.5, bf16[2048,128]{1,0:T(8,128)(2,1)} %bitcast.3, bf16[1024,128]{1,0:T(8,128)(2,1)} %bitcast.4, bf16[1024,2048]{1,0:T(8,128)(2,1)} %w_hbm.1, s32[64]{0:T(128)} %parents.1, s32[64]{0:T(128)} %own_len.1, s32[64]{0:T(128)} %first_beam.1), custom_call_target="tpu_custom_call" | custom-call | tf_op jit(solution)/shard_map/pallas_call | solution.py:281
  17.4 1.3 %copy.10 = bf16[8,512]{1,0:T(8,128)(2,1)} copy(bf16[8,512]{1,0:T(8,128)(2,1)} %shard_map.82) | data formatting | bytes 16384

commit v3 on v2

--- a/solution.py
+++ b/solution.py
@@ -147,28 +147,39 @@
         for c in range(per_dev):
             s = jnp.where(rel == c, nt(q, kb[pl.ds(c * cache, cache), :]), s)
         s = jnp.where(lanes < length, s, NEG)
+        ahead = [delta for delta in deltas if delta >= 0]
+        reach = rows * len(ahead)
+        gap = spread(ahead, 2)
+        mine = (gap >= 0) & (gap < per_dev)
         prompt = []
-        if min(deltas) >= 0:
-            gap = spread(deltas, 2)
-            mine = (gap >= 0) & (gap < per_dev)
-            for c in range(n_prompt // HD):
-                sp = nt(q, kb[pl.ds(n_own + c * HD, HD), :])
-                prompt.append(jnp.where(mine, sp, NEG))
-        top = functools.reduce(jnp.maximum, prompt, s)
+        for c in range(n_prompt // HD):
+            sp = nt(q[:reach], kb[pl.ds(n_own + c * HD, HD), :])
+            prompt.append(jnp.where(mine, sp, NEG))
+
+        def join(head, tail):
+            return jnp.concatenate([head, tail[reach:]], axis=0) if reach < tail.shape[0] else head
+
+        top = join(functools.reduce(jnp.maximum, prompt, s[:reach]), s)
         m = jnp.max(top, axis=1, keepdims=True)
         if fresh is not None:
             m = jnp.maximum(m, fresh)
         p = jnp.exp((s - m) * scale)
-        weights = [jnp.exp((sp - m) * scale).astype(jnp.bfloat16) for sp in prompt]
+        weights = [jnp.exp((sp - m[:reach]) * scale).astype(jnp.bfloat16) for sp in prompt]
+        kept = p.astype(jnp.bfloat16).astype(jnp.float32)
         total = functools.reduce(
-            jnp.add,
-            [x.astype(jnp.float32) for x in weights],
-            p.astype(jnp.bfloat16).astype(jnp.float32),
-        )
-        total = jnp.sum(total, axis=1, keepdims=True)
+            jnp.add, [x.astype(jnp.float32) for x in weights], kept[:reach]
+        )
+        total = jnp.sum(join(total, kept), axis=1, keepdims=True)
         picked = [jnp.where(rel == c, p, 0.0).astype(jnp.bfloat16) for c in range(per_dev)]
-        table = jnp.concatenate(picked + weights, axis=1)
-        w = jnp.dot(table, vb[pl.ds(0, table.shape[1]), :], preferred_element_type=jnp.float32)
+        w = jnp.dot(
+            jnp.concatenate(picked, axis=1), vb[pl.ds(0, n_own), :],
+            preferred_element_type=jnp.float32,
+        )
+        w_prompt = jnp.dot(
+            jnp.concatenate(weights, axis=1), vb[pl.ds(n_own, n_prompt), :],
+            preferred_element_type=jnp.float32,
+        )
+        w = join(w[:reach] + w_prompt, w)
         return m, total, w
 
     k_tiled = jnp.concatenate([new_k] * groups, axis=0)
@@ -179,30 +190,27 @@
     l0 = l0 + pf
     w0 = w0 + pf * v_tiled
 
-    for pair in (0, 1):
-        deltas = NEAR[2 * pair:2 * pair + 2]
-        for k in (2 * pair, 2 * pair + 1):
-            @pl.when(there(NEAR[k]))
-            def _():
-                q_copy(k, d + NEAR[k]).wait_recv()
-        m, total, w = attend(qin[pl.ds(2 * pair * rows, 2 * rows), :], deltas)
-        lanes = lax.broadcasted_iota(jnp.int32, w.shape, 1)
-        stats = jnp.zeros(w.shape, jnp.float32)
-        at = 0
-        for value, count in ((m, 3), (total, 2)):
-            left = value
-            for _ in range(count):
-                piece = left.astype(jnp.bfloat16).astype(jnp.float32)
-                left = left - piece
-                stats = jnp.where(lanes == at, piece, stats)
-                at += 1
-        for i in (0, 1):
-            k = 2 * pair + i
-            res[k, :, pl.ds(0, HD)] = w[i * rows:(i + 1) * rows].astype(jnp.bfloat16)
-            res[k, :, pl.ds(HD, HD)] = stats[i * rows:(i + 1) * rows].astype(jnp.bfloat16)
-            @pl.when(there(NEAR[k]))
-            def _():
-                r_copy(k, NEAR.index(-NEAR[k]), d + NEAR[k]).start()
+    for k, delta in enumerate(NEAR):
+        @pl.when(there(delta))
+        def _():
+            q_copy(k, d + delta).wait_recv()
+    m, total, w = attend(qin[...], NEAR)
+    lanes = lax.broadcasted_iota(jnp.int32, w.shape, 1)
+    stats = jnp.zeros(w.shape, jnp.float32)
+    at = 0
+    for value, count in ((m, 3), (total, 2)):
+        left = value
+        for _ in range(count):
+            piece = left.astype(jnp.bfloat16).astype(jnp.float32)
+            left = left - piece
+            stats = jnp.where(lanes == at, piece, stats)
+            at += 1
+    for k, delta in enumerate(NEAR):
+        res[k, :, pl.ds(0, HD)] = w[k * rows:(k + 1) * rows].astype(jnp.bfloat16)
+        res[k, :, pl.ds(HD, HD)] = stats[k * rows:(k + 1) * rows].astype(jnp.bfloat16)
+        @pl.when(there(delta))
+        def _():
+            r_copy(k, NEAR.index(-delta), d + delta).start()
 
     parts = [(m0, l0, w0)]
     for k, delta in enumerate(NEAR):

time: 18.9 us -> 18.4 us (0.974)
  Pallas kernels: 17.4 us -> 16.9 us
    pallas_call x1, Pallas kernels: 17.4 us -> 16.9 us  [local(): pl.pallas_call(functools.partial(kernel, n, n_tp), out_shape=jax.ShapeDty...]
where the time goes in v3:
time: 18.4 us; the launch traced here: 18.2 us
  Pallas kernels  16.9 us (92%)
  local copies, waits for them, and re-layouts  1.3 us (7%)
    pallas_call x1, Pallas kernels, local(): pl.pallas_call(functools.partial(kernel, n, n_tp), out_shape=jax.ShapeDty...  16.9 us
    unnamed x1, local copies, waits for them, and re-layouts  1.3 us

profile of v3, /device:TPU:0, one launch (start us, length us, event | category | flops | bytes accessed | tf_op | source)
XLA Modules:
  0.0 18.2 jit_solution(1818162362255791130)
XLA Ops:
  0.0 16.9 %shard_map.82 = bf16[8,512]{1,0:T(8,128)(2,1)} custom-call(bf16[8,1024]{1,0:T(8,128)(2,1)} %q_ref.1, bf16[16,128]{1,0:T(8,128)(2,1)} %bitcast.5, bf16[2048,128]{1,0:T(8,128)(2,1)} %bitcast.3, bf16[1024,128]{1,0:T(8,128)(2,1)} %bitcast.4, bf16[1024,2048]{1,0:T(8,128)(2,1)} %w_hbm.1, s32[64]{0:T(128)} %parents.1, s32[64]{0:T(128)} %own_len.1, s32[64]{0:T(128)} %first_beam.1), custom_call_target="tpu_custom_call" | custom-call | tf_op jit(solution)/shard_map/pallas_call | solution.py:289
  16.9 1.3 %copy.10 = bf16[8,512]{1,0:T(8,128)(2,1)} copy(bf16[8,512]{1,0:T(8,128)(2,1)} %shard_map.82) | data formatting | bytes 16384

commit v4 on v3

--- a/solution.py
+++ b/solution.py
@@ -19,6 +19,12 @@
     return lax.dot_general(
         a, b, (((1,), (1,)), ((), ())), preferred_element_type=jnp.float32
     )
+
+
+def eye(count):
+    i = lax.broadcasted_iota(jnp.int32, (count, HD), 0)
+    j = lax.broadcasted_iota(jnp.int32, (count, HD), 1)
+    return jnp.where(i == j, 1.0, 0.0).astype(jnp.bfloat16)
 
 
 def kernel(
@@ -206,8 +212,12 @@
             stats = jnp.where(lanes == at, piece, stats)
             at += 1
     for k, delta in enumerate(NEAR):
-        res[k, :, pl.ds(0, HD)] = w[k * rows:(k + 1) * rows].astype(jnp.bfloat16)
-        res[k, :, pl.ds(HD, HD)] = stats[k * rows:(k + 1) * rows].astype(jnp.bfloat16)
+        res[k, pl.ds(0, rows), :] = w[k * rows:(k + 1) * rows].astype(jnp.bfloat16)
+        flipped = lax.dot_general(
+            stats[k * rows:(k + 1) * rows].astype(jnp.bfloat16), eye(rows),
+            (((0,), (0,)), ((), ())), preferred_element_type=jnp.float32,
+        )
+        res[k, pl.ds(rows, 16), :] = flipped[:16].astype(jnp.bfloat16)
         @pl.when(there(delta))
         def _():
             r_copy(k, NEAR.index(-delta), d + delta).start()
@@ -217,8 +227,11 @@
         @pl.when(there(delta))
         def _():
             r_copy(k, k, d + delta).wait_recv()
-        w = rin[k, :, pl.ds(0, HD)].astype(jnp.float32)
-        st = rin[k, :, pl.ds(HD, HD)].astype(jnp.float32)
+        w = rin[k, pl.ds(0, rows), :].astype(jnp.float32)
+        st = lax.dot_general(
+            rin[k, pl.ds(rows, 16), :], eye(16),
+            (((0,), (0,)), ((), ())), preferred_element_type=jnp.float32,
+        )[:rows]
         m = st[:, 0:1] + st[:, 1:2] + st[:, 2:3]
         l = st[:, 3:4] + st[:, 4:5]
         m = jnp.where(there(delta), m, NEG)
@@ -300,8 +313,8 @@
             pltpu.VMEM((total // 2, HD), bf16),
             pltpu.VMEM((total // 2, HD), bf16),
             pltpu.VMEM(out_weight.shape, bf16),
-            pltpu.VMEM((near, rows, 2 * HD), bf16),
-            pltpu.VMEM((near, rows, 2 * HD), bf16),
+            pltpu.VMEM((near, rows + 16, HD), bf16),
+            pltpu.VMEM((near, rows + 16, HD), bf16),
             pltpu.VMEM((n_tp - 1, 2 * per_dev, width // 2), bf16),
             pltpu.VMEM((n_tp - 1, 2 * per_dev, width // 2), bf16),
             dma((3,)),

time: 18.4 us -> 18.8 us (1.022)
  Pallas kernels: 16.9 us -> 17.2 us
    pallas_call x1, Pallas kernels: 16.9 us -> 17.2 us  [local(): pl.pallas_call(functools.partial(kernel, n, n_tp), out_shape=jax.ShapeDty...]
where the time goes in v4:
time: 18.8 us; the launch traced here: 18.5 us
  Pallas kernels  17.2 us (91%)
  local copies, waits for them, and re-layouts  1.3 us (7%)
    pallas_call x1, Pallas kernels, local(): pl.pallas_call(functools.partial(kernel, n, n_tp), out_shape=jax.ShapeDty...  17.2 us
    unnamed x1, local copies, waits for them, and re-layouts  1.3 us

profile of v4, /device:TPU:0, one launch (start us, length us, event | category | flops | bytes accessed | tf_op | source)
XLA Modules:
  0.0 18.5 jit_solution(5565599599735603090)
XLA Ops:
  0.0 17.2 %shard_map.82 = bf16[8,512]{1,0:T(8,128)(2,1)} custom-call(bf16[8,1024]{1,0:T(8,128)(2,1)} %q_ref.1, bf16[16,128]{1,0:T(8,128)(2,1)} %bitcast.5, bf16[2048,128]{1,0:T(8,128)(2,1)} %bitcast.3, bf16[1024,128]{1,0:T(8,128)(2,1)} %bitcast.4, bf16[1024,2048]{1,0:T(8,128)(2,1)} %w_hbm.1, s32[64]{0:T(128)} %parents.1, s32[64]{0:T(128)} %own_len.1, s32[64]{0:T(128)} %first_beam.1), custom_call_target="tpu_custom_call" | custom-call | tf_op jit(solution)/shard_map/pallas_call | solution.py:302
  17.2 1.3 %copy.10 = bf16[8,512]{1,0:T(8,128)(2,1)} copy(bf16[8,512]{1,0:T(8,128)(2,1)} %shard_map.82) | data formatting | bytes 16384
